TPU v7x, 32 devices: a whole 2x2x4 slice. The times are simulated.
32 devices in a mesh: groups: 2 (over y), dp: 4 (over z), tensor: 4 (over x, core).
Axes of the slice: x: 2, y: 2, z: 4, core: 2. Of those that a mesh axis runs over, the one named last changes fastest.
Arguments:
- residual: bfloat16 [8192, 3072], P(('groups', 'dp'), 'tensor'), parts along dimension 0, may hold values from -6 to 6
- attention: bfloat16 [8192, 3072], P(('groups', 'dp'), 'tensor'), parts along dimension 0, may hold values from -6 to 6
- gate: bfloat16 [128, 3072], P(('groups', 'dp'), 'tensor'), parts along dimension 0, may hold values from 0.5 to 1.5
- output_projection_weight: bfloat16 [3072, 3072], P(None, 'tensor'), may hold values from -0.109375 to 0.109375
- adapter_down_weight: bfloat16 [32, 64, 3072], P('dp', None, 'tensor'), may hold values from -0.109375 to 0.109375
- adapter_up_weight: bfloat16 [32, 64, 3072], P('dp', None, 'tensor'), may hold values from -0.75 to 0.75
- request_adapter_index: int32 [128], P(('groups', 'dp')), parts along dimension 0, may hold values from 0 to 31, as said below
Outputs:
- updated: bfloat16 [8192, 3072], P(('groups', 'dp'), 'tensor'), parts along dimension 0
There are 2 independent parts, one for each index of `groups`. A program takes and returns all parts, laid end to end along the dimension named above; an argument that names none is the same for every part. Nothing has to cross between parts.
Inputs may be any that keep to these rules, and one draw needn't show every extreme that they name: `request_adapter_index`: at most 8 of the requests of one index of dp use adapters held by one index of dp; in every draw one index of dp holds the adapters of exactly 8 requests of every index of dp.
All inputs are finite; a program needn't handle non-finite values.
Results may differ from a plain program's by a relative error of at most 0.0043.
Values may be sent and summed in bfloat16 or wider, within the bound.
A program may use at most 128 MiB of HBM per device.

v0:
```python
import jax
import jax.numpy as jnp
from jax import lax
from jax.sharding import PartitionSpec as P


def body(
    residual,
    attention,
    gate,
    output_projection_weight,
    adapter_down_weight,
    adapter_up_weight,
    request_adapter_index,
):
    rows, width = attention.shape
    req_dev = request_adapter_index.shape[0]
    window = rows // req_dev
    holders = lax.axis_size("dp")
    adapter_device_share = adapter_down_weight.shape[0]
    capacity = max(1, 2 * req_dev // holders)
    total = holders * capacity
    owner = request_adapter_index // adapter_device_share
    local = request_adapter_index % adapter_device_share
    same_owner = owner[:, None] == owner[None, :]
    earlier = jnp.arange(req_dev)[None, :] < jnp.arange(req_dev)[:, None]
    place = jnp.sum(jnp.logical_and(same_owner, earlier).astype(jnp.int32), axis=1)
    target = owner * capacity + place
    onehot = jnp.arange(total)[:, None] == target[None, :]
    chosen = onehot.astype(jnp.bfloat16)
    flat = attention.reshape(req_dev, window * width)
    packed = jnp.dot(chosen, flat, preferred_element_type=jnp.float32).astype(jnp.bfloat16)
    packed = packed.reshape(holders, capacity, window, width)
    wanted = jnp.sum(onehot.astype(jnp.int32) * local[None, :], axis=1)
    wanted = wanted.reshape(holders, capacity)
    got_rows = lax.all_to_all(packed, "dp", split_axis=0, concat_axis=0, tiled=True)
    received_slots = lax.all_to_all(wanted, "dp", split_axis=0, concat_axis=0, tiled=True)
    down_matrix = jnp.take(adapter_down_weight, received_slots, axis=0)
    up_matrix = jnp.take(adapter_up_weight, received_slots, axis=0)
    partial_low = jnp.einsum(
        "ncwf,ncrf->ncwr", got_rows, down_matrix, preferred_element_type=jnp.float32
    )
    array_shape = partial_low.shape
    summed = lax.psum(
        partial_low.reshape(array_shape[0], array_shape[1], array_shape[2] * array_shape[3]),
        "tensor",
    )
    low = summed.reshape(array_shape).astype(jnp.bfloat16)
    delta = jnp.einsum(
        "ncwr,ncrf->ncwf", low, up_matrix, preferred_element_type=jnp.float32
    ).astype(jnp.bfloat16)
    returned = lax.all_to_all(delta, "dp", split_axis=0, concat_axis=0, tiled=True)
    gathered_back = jnp.dot(
        chosen.T, returned.reshape(total, window * width), preferred_element_type=jnp.float32
    )
    delta_rows = gathered_back.reshape(rows, width)
    base = jnp.dot(
        lax.all_gather(attention, "tensor", axis=1, tiled=True),
        output_projection_weight,
        preferred_element_type=jnp.float32,
    )
    scale = jnp.repeat(gate, window, axis=0).astype(jnp.float32)
    updated = residual.astype(jnp.float32) + scale * (base + delta_rows)
    return updated.astype(jnp.bfloat16)


def solution(mesh):
    in_specs = (
        P(("groups", "dp"), "tensor"),
        P(("groups", "dp"), "tensor"),
        P(("groups", "dp"), "tensor"),
        P(None, "tensor"),
        P("dp", None, "tensor"),
        P("dp", None, "tensor"),
        P(("groups", "dp")),
    )
    out_specs = P(("groups", "dp"), "tensor")
    return jax.shard_map(body, mesh=mesh, in_specs=in_specs, out_specs=out_specs, check_vma=False)
```

profile of v0, /device:TPU:0, one launch (start us, length us, event | category | flops | bytes accessed | tf_op | source)
XLA Modules:
  0.0 223.5 jit_solution(13054233354045331101)
XLA Ops:
  6.5 0.0 copy-start
  6.5 0.7 and_select_fusion
  7.3 0.2 convert_reduce_fusion
  7.5 0.1 select_reduce_fusion
  7.6 0.7 all_to_all.15
  8.2 6.3 %all-to-all-start.1 = ((s32[4,1,8]{2,1,0:T(1,128)}), s32[4,1,8]{2,1,0:T(1,128)S(1)}, u32[]{:S(2)}, u32[]{:S(2)}) async-start(s32[4,1,8]{2,1,0:T(1,128)} %bitcast.2), calls=%async_computation.1 | async-start | bytes 4096 | tf_op jit(solution)/shard_map/all_to_all | solution.py:37
  14.5 1.9 reshape.32
  16.4 1.1 convolution_convert_fusion
  17.5 2.4 %copy.11 = bf16[4,8,64,768]{3,2,1,0:T(8,128)(2,1)} copy(bf16[4,8,64,768]{3,1,2,0:T(8,128)(2,1)S(1)} %bitcast.24) | data formatting | bytes 6291456 | tf_op jit(solution)/shard_map/reshape | solution.py:33
  19.9 0.1 all-to-all-done.1
  20.0 5.0 %all-to-all-start = ((bf16[4,8,64,768]{3,2,1,0:T(8,128)(2,1)}), bf16[4,8,64,768]{3,2,1,0:T(8,128)(2,1)}, u32[]{:S(2)}, u32[]{:S(2)}) async-start(bf16[4,8,64,768]{3,2,1,0:T(8,128)(2,1)} %copy.11), calls=%async_computation | async-start | bytes 6291456 | tf_op jit(solution)/shard_map/all_to_all | solution.py:36
  25.0 0.0 all-gather.2.cloned.1.call-start
  25.0 0.7 all-gather.2.cloned.1.call-update
  25.7 0.1 reshape.57
  25.8 0.0 copy-done
  25.8 0.0 copy-start.1
  25.8 2.4 %gather_fusion = bf16[32,64,768]{2,1,0:T(8,128)(2,1)} fusion(bf16[8,64,768]{2,1,0:T(8,128)(2,1)S(1)} %copy-done, s32[1024]{0:T(1024)S(1)} %pad_clamp_fusion), kind=kCustom, calls=%fused_computation.clone | custom fusion | bytes 6291584 | tf_op jit(solution)/shard_map/jit(_take)/gather | solution.py:38
  28.2 0.0 copy-done.1
  28.2 2.4 %gather_fusion.1 = bf16[32,64,768]{2,1,0:T(8,128)(2,1)} fusion(bf16[8,64,768]{2,1,0:T(8,128)(2,1)S(1)} %copy-done.1, s32[1024]{0:T(1024)S(1)} %pad_clamp_fusion), kind=kCustom, calls=%fused_computation.1.clone | custom fusion | bytes 6291584 | tf_op jit(solution)/shard_map/jit(_take)/gather | solution.py:39
  30.6 64.8 %all-to-all-done = bf16[4,8,64,768]{3,2,1,0:T(8,128)(2,1)} async-done(((bf16[4,8,64,768]{3,2,1,0:T(8,128)(2,1)}), bf16[4,8,64,768]{3,2,1,0:T(8,128)(2,1)}, u32[]{:S(2)}, u32[]{:S(2)}) %all-to-all-start) | async-done | bytes 3145760 | tf_op jit(solution)/shard_map/all_to_all | solution.py:36
  95.4 3.9 %fusion.4 = f32[4,8,64,64]{3,2,1,0:T(8,128)S(1)} fusion(bf16[4,8,64,768]{3,2,1,0:T(8,128)(2,1)} %all-to-all-done, bf16[4,8,64,768]{3,2,1,0:T(8,128)(2,1)} %bitcast.25, pred[4,8]{1,0:T(4,128)(4,1)S(1)} %compare_and_fusion), kind=kOutput, calls=%fused_computation.8 | convolution fusion | flops 202899456 | bytes 6815776 | tf_op jit(solution)/shard_map/ncwf,ncrf->ncwr/dot_general | solution.py:40
  99.2 0.4 reshape.34
  99.6 16.6 %all-reduce.1 = bf16[4,8,4096]{2,1,0:T(8,128)(2,1)S(1)} all-reduce(f32[4,8,4096]{2,1,0:T(8,128)S(1)} %reshape.34), channel_id=1, replica_groups=mesh['groups'=2,'dp'=4,'tensor'=4] {'tensor'}, use_global_device_ids=true, to_apply=%region_2.4 | all-reduce | flops 131072 | bytes 786432 | tf_op jit(solution)/shard_map/psum | solution.py:44
  116.2 0.5 convert_element_type.36
  116.8 4.6 %fusion.8 = bf16[4,8,64,768]{3,2,1,0:T(8,128)(2,1)} fusion(bf16[4,8,64,64]{3,2,1,0:T(8,128)(2,1)S(1)} %convert_element_type.36, bf16[4,8,64,768]{3,2,1,0:T(8,128)(2,1)} %bitcast.22, pred[4,8]{1,0:T(4,128)(4,1)S(1)} %compare_and_fusion), kind=kOutput, calls=%fused_computation.12 | convolution fusion | flops 204472320 | bytes 6553632 | tf_op jit(solution)/shard_map/ncwr,ncrf->ncwf/dot_general | solution.py:49
  121.4 0.0 copy-start.2
  121.4 4.8 %all-to-all-start.2 = ((bf16[4,8,64,768]{3,2,1,0:T(8,128)(2,1)}), bf16[4,8,64,768]{3,2,1,0:T(8,128)(2,1)}, u32[]{:S(2)}, u32[]{:S(2)}) async-start(bf16[4,8,64,768]{3,2,1,0:T(8,128)(2,1)} %fusion.8), calls=%async_computation.2 | async-start | bytes 6291456 | tf_op jit(solution)/shard_map/all_to_all | solution.py:52
  126.2 0.0 copy-done.2
  126.2 71.2 %all-to-all-done.2 = bf16[4,8,64,768]{3,2,1,0:T(8,128)(2,1)} async-done(((bf16[4,8,64,768]{3,2,1,0:T(8,128)(2,1)}), bf16[4,8,64,768]{3,2,1,0:T(8,128)(2,1)}, u32[]{:S(2)}, u32[]{:S(2)}) %all-to-all-start.2) | async-done | bytes 3145760 | tf_op jit(solution)/shard_map/all_to_all | solution.py:52
  197.4 3.6 %copy.13 = bf16[4,8,64,768]{3,1,2,0:T(8,128)(2,1)S(1)} copy(bf16[4,8,64,768]{3,2,1,0:T(8,128)(2,1)} %all-to-all-done.2) | data formatting | bytes 6291456
  201.0 2.3 %fusion.13 = f32[16,49152]{1,0:T(8,128)} fusion(bf16[32,49152]{1,0:T(8,128)(2,1)S(1)} %bitcast.23, s32[16]{0:T(128)S(1)} %multiply_add_fusion), kind=kOutput, calls=%fused_computation.19 | convolution fusion | flops 50332160 | bytes 6291520 | tf_op jit(solution)/shard_map/dot_general | solution.py:53
  203.3 0.0 copy-start.3
  203.3 3.5 %reshape.36 = f32[1024,768]{1,0:T(8,128)} reshape(f32[16,49152]{1,0:T(8,128)} %fusion.13) | data formatting | bytes 6291456 | tf_op jit(solution)/shard_map/reshape | solution.py:56
  206.8 0.0 all-gather.2.cloned.1.call-done
  206.8 0.0 copy-done.3
  206.8 9.9 %fusion.1 = bf16[1024,768]{1,0:T(8,128)(2,1)} fusion(f32[1024,768]{1,0:T(8,128)} %reshape.36, bf16[1024,768]{1,0:T(8,128)(2,1)S(1)} %copy-done.3, bf16[1024,3072]{1,0:T(8,128)(2,1)} %all-gather.2.cloned.1.call-done, bf16[3072,768]{1,0:T(8,128)(2,1)} %param.12, f32[16,768]{1,0:T(8,128)S(1)} %convert_element_type.31), kind=kOutput, calls=%fused_computation.5 | convolution fusion | flops 4835770368 | bytes 17350656 | tf_op jit(solution)/shard_map/dot_general | solution.py:57
  (5 shorter events, 0.0 us)
Async XLA Ops:
  6.5 19.3 %copy-start = (bf16[8,64,768]{2,1,0:T(8,128)(2,1)S(1)}, bf16[8,64,768]{2,1,0:T(8,128)(2,1)}, u32[]{:S(2)}) copy-start(bf16[8,64,768]{2,1,0:T(8,128)(2,1)} %param.13) | copy-start | bytes 2359300
  8.2 11.8 %all-to-all-start.1 = ((s32[4,1,8]{2,1,0:T(1,128)}), s32[4,1,8]{2,1,0:T(1,128)S(1)}, u32[]{:S(2)}, u32[]{:S(2)}) async-start(s32[4,1,8]{2,1,0:T(1,128)} %bitcast.2), calls=%async_computation.1 | async-start | bytes 4096 | tf_op jit(solution)/shard_map/all_to_all | solution.py:37
  20.0 75.3 %all-to-all-start = ((bf16[4,8,64,768]{3,2,1,0:T(8,128)(2,1)}), bf16[4,8,64,768]{3,2,1,0:T(8,128)(2,1)}, u32[]{:S(2)}, u32[]{:S(2)}) async-start(bf16[4,8,64,768]{3,2,1,0:T(8,128)(2,1)} %copy.11), calls=%async_computation | async-start | bytes 6291456 | tf_op jit(solution)/shard_map/all_to_all | solution.py:36
  25.0 181.8 %all-gather.2.cloned.1.call-start = ((), (), s32[]{:S(2)}) async-start(), calls=%async_computation.3 | async-start | bytes 7864320 | tf_op jit(solution)/shard_map/all_gather | solution.py:58
  25.8 2.4 %copy-start.1 = (bf16[8,64,768]{2,1,0:T(8,128)(2,1)S(1)}, bf16[8,64,768]{2,1,0:T(8,128)(2,1)}, u32[]{:S(2)}) copy-start(bf16[8,64,768]{2,1,0:T(8,128)(2,1)} %param.14) | copy-start | bytes 2359300
  121.4 4.8 %copy-start.2 = (bf16[16,768]{1,0:T(8,128)(2,1)S(1)}, bf16[16,768]{1,0:T(8,128)(2,1)}, u32[]{:S(2)}) copy-start(bf16[16,768]{1,0:T(8,128)(2,1)} %param.11) | copy-start | bytes 73732
  121.4 76.0 %all-to-all-start.2 = ((bf16[4,8,64,768]{3,2,1,0:T(8,128)(2,1)}), bf16[4,8,64,768]{3,2,1,0:T(8,128)(2,1)}, u32[]{:S(2)}, u32[]{:S(2)}) async-start(bf16[4,8,64,768]{3,2,1,0:T(8,128)(2,1)} %fusion.8), calls=%async_computation.2 | async-start | bytes 6291456 | tf_op jit(solution)/shard_map/all_to_all | solution.py:52
  203.3 3.5 %copy-start.3 = (bf16[1024,768]{1,0:T(8,128)(2,1)S(1)}, bf16[1024,768]{1,0:T(8,128)(2,1)}, u32[]{:S(2)}) copy-start(bf16[1024,768]{1,0:T(8,128)(2,1)} %param.9) | copy-start | bytes 4718596
Sparse Core Ops, SparseCore 0:
  27.3 47.8 all-gather.1
where the time goes:
time: 224 us
  waiting for transfers between devices  137 us (61%)
  matrix products  21.8 us (10%)
  local copies, waits for them, and re-layouts  17.8 us (8%)
  blocking collectives  16.6 us (7%)
  starting transfers between devices  16 us (7%)
  between operations  13.5 us (6%)
    all_to_all x1, waiting for transfers between devices, body(): lax.all_to_all(delta, 'dp', split_axis=0, concat_axis=0, tiled=True)  71.2 us
    all_to_all x1, waiting for transfers between devices, body(): lax.all_to_all(packed, 'dp', split_axis=0, concat_axis=0, tiled=True)  64.8 us
    psum x1, blocking collectives, body(): lax.psum(partial_low.reshape(array_shape[0], array_shape[1], array_shape[...  16.6 us
    dot_general x1, matrix products, body(): jnp.dot(lax.all_gather(attention, 'tensor', axis=1, tiled=True), output_p...  9.93 us
    all_to_all x1, starting transfers between devices, body(): lax.all_to_all(wanted, 'dp', split_axis=0, concat_axis=0, tiled=True)  6.32 us
    all_to_all x1, starting transfers between devices, body(): lax.all_to_all(packed, 'dp', split_axis=0, concat_axis=0, tiled=True)  4.95 us
    all_to_all x1, starting transfers between devices, body(): lax.all_to_all(delta, 'dp', split_axis=0, concat_axis=0, tiled=True)  4.76 us
    dot_general x1, matrix products, body(): jnp.einsum('ncwr,ncrf->ncwf', low, up_matrix, preferred_element_type=jnp....  4.62 us
  transfers between devices with their start and end apart: 4, of which 3 were waited for; matrix products, arithmetic and copies ran while one was open for 13% of the time, Pallas kernels for 0%

commit v1 on v0

--- a/solution.py
+++ b/solution.py
@@ -1,10 +1,18 @@
+import functools
+
 import jax
 import jax.numpy as jnp
 from jax import lax
+from jax.experimental import pallas as pl
+from jax.experimental.pallas import tpu as pltpu
 from jax.sharding import PartitionSpec as P
 
-
-def body(
+MESH = pl.DeviceIdType.MESH
+PIECES = 2
+PARTS = 4
+
+
+def exchange_body(
     residual,
     attention,
     gate,
@@ -64,6 +72,395 @@
     return updated.astype(jnp.bfloat16)
 
 
+def fused_kernel(
+    holders,
+    index,
+    gate_in,
+    residual_in,
+    attention_in,
+    weight_in,
+    down_in,
+    up_in,
+    out,
+    attention,
+    weight,
+    down,
+    up,
+    residual,
+    gate,
+    total,
+    result,
+    partial,
+    arrived,
+    low,
+    z_send,
+    z_recv,
+    y_send,
+    y_recv,
+    x_send,
+    x_recv,
+    near_send,
+    near_recv,
+    pass_send,
+    pass_recv,
+    sum_send,
+    sum_recv,
+    low_send,
+    low_recv,
+    local_sem,
+    out_sem,
+):
+    g = lax.axis_index("groups")
+    d = lax.axis_index("dp")
+    t = lax.axis_index("tensor")
+    core = lax.rem(t, 2)
+    sibling = t + 1 - 2 * core
+    across = lax.rem(t + 2, 4)
+    diagonal = lax.rem(sibling + 2, 4)
+
+    rows, width = attention_in.shape
+    requests = gate_in.shape[0]
+    window = rows // requests
+    share, rank, _ = down_in.shape
+    half = share // 2
+    piece = half // PIECES
+    part_rows = rows // PARTS
+    pairs = requests // 2
+    own_pairs = pairs // 4
+    hops = holders - 1
+    inputs, buffers = (down_in, up_in), (down, up)
+
+    own_block = pl.ds(d * share, share)
+    local = [
+        pltpu.make_async_copy(src, dst, local_sem.at[i])
+        for i, (src, dst) in enumerate(
+            [
+                (attention_in, attention.at[t]),
+                (down_in, down.at[own_block]),
+                (weight_in, weight),
+                (residual_in, residual),
+                (up_in, up.at[own_block]),
+            ]
+        )
+    ]
+
+    barrier = pltpu.get_barrier_semaphore()
+
+    def greet(where):
+        pl.semaphore_signal(barrier, inc=1, device_id=where, device_id_type=MESH)
+
+    for step in (1, 2, 3):
+        greet({"tensor": lax.rem(t + step, 4)})
+    greet({"groups": 1 - g})
+
+    @pl.when(d > 0)
+    def _():
+        greet({"dp": d - 1})
+
+    @pl.when(d < holders - 1)
+    def _():
+        greet({"dp": d + 1})
+
+    for copy in local:
+        copy.start()
+    pl.semaphore_wait(barrier, 4 + (d > 0).astype(jnp.int32) + (d < holders - 1).astype(jnp.int32))
+
+    def slot(stage, way, hop, j):
+        return ((stage * 2 + way) * hops + hop) * PIECES + j
+
+    def place(holder, side, j):
+        return pl.ds(holder * share + side * half + j * piece, piece)
+
+    def rank_on(way):
+        return d if way == 0 else holders - 1 - d
+
+    def sends(way, hop):
+        e = rank_on(way)
+        return jnp.logical_and(e < holders - 1, e >= hop)
+
+    def receives(way, hop):
+        return rank_on(way) > hop
+
+    def z_copy(stage, way, hop, j):
+        sign = 1 if way == 0 else -1
+        target = buffers[stage].at[place(d - sign * hop, g, j)]
+        source = inputs[stage].at[pl.ds(g * half + j * piece, piece)] if hop == 0 else target
+        i = slot(stage, way, hop, j)
+        return pltpu.make_async_remote_copy(
+            src_ref=source, dst_ref=target, send_sem=z_send.at[i], recv_sem=z_recv.at[i],
+            device_id={"dp": d + sign}, device_id_type=MESH,
+        )
+
+    def z_arrival(stage, way, hop, j):
+        sign = 1 if way == 0 else -1
+        target = buffers[stage].at[place(d - sign * (hop + 1), g, j)]
+        i = slot(stage, way, hop, j)
+        return pltpu.make_async_remote_copy(
+            src_ref=target, dst_ref=target, send_sem=z_send.at[i], recv_sem=z_recv.at[i],
+            device_id={"dp": d - sign}, device_id_type=MESH,
+        )
+
+    def y_copy(stage, way, hop, j, side):
+        sign = 1 if way == 0 else -1
+        target = buffers[stage].at[place(d - sign * (hop + 1), side, j)]
+        i = slot(stage, way, hop, j)
+        return pltpu.make_async_remote_copy(
+            src_ref=target, dst_ref=target, send_sem=y_send.at[i], recv_sem=y_recv.at[i],
+            device_id={"groups": 1 - g}, device_id_type=MESH,
+        )
+
+    def start_own(stage):
+        for j in range(PIECES):
+            for way in (0, 1):
+                @pl.when(sends(way, 0))
+                def _():
+                    z_copy(stage, way, 0, j).start()
+
+    def relay(stage, hop, j):
+        for way in (0, 1):
+            @pl.when(receives(way, hop))
+            def _():
+                z_arrival(stage, way, hop, j).wait_recv()
+                if hop + 1 < hops:
+                    @pl.when(sends(way, hop + 1))
+                    def _():
+                        z_copy(stage, way, hop + 1, j).start()
+                y_copy(stage, way, hop, j, g).start()
+
+    def await_other_group(stage):
+        for hop in range(hops):
+            for j in range(PIECES):
+                for way in (0, 1):
+                    @pl.when(receives(way, hop))
+                    def _():
+                        y_copy(stage, way, hop, j, 1 - g).wait_recv()
+
+    def part(q):
+        return pl.ds(q * part_rows, part_rows)
+
+    def attention_copy(source, which, q, send, recv, to):
+        return pltpu.make_async_remote_copy(
+            src_ref=source, dst_ref=attention.at[which, part(q)],
+            send_sem=send.at[q], recv_sem=recv.at[q],
+            device_id={"tensor": to}, device_id_type=MESH,
+        )
+
+    def across_copy(q):
+        return attention_copy(attention_in.at[part(q)], t, q, x_send, x_recv, across)
+
+    def near_copy(q):
+        return attention_copy(attention_in.at[part(q)], t, q, near_send, near_recv, sibling)
+
+    def pass_copy(q):
+        return attention_copy(attention.at[across, part(q)], across, q, pass_send, pass_recv, sibling)
+
+    def relay_attention(q):
+        attention_copy(attention.at[across, part(q)], across, q, x_send, x_recv, across).wait_recv()
+        pass_copy(q).start()
+
+    tile = 256
+
+    def base_part(q):
+        attention_copy(attention.at[sibling, part(q)], sibling, q, near_send, near_recv, sibling).wait_recv()
+        attention_copy(attention.at[diagonal, part(q)], diagonal, q, pass_send, pass_recv, sibling).wait_recv()
+
+        def columns(n, carry):
+            cols = pl.ds(pl.multiple_of(n * tile, tile), tile)
+            acc = None
+            for s in range(4):
+                term = jnp.dot(
+                    attention[s, part(q), :],
+                    weight[pl.ds(s * width, width), cols],
+                    preferred_element_type=jnp.float32,
+                )
+                acc = term if acc is None else acc + term
+            for i in range(part_rows // window):
+                r = q * (part_rows // window) + i
+                at = pl.ds(r * window, window)
+                total[at, cols] = (
+                    residual[at, cols].astype(jnp.float32)
+                    + gate[pl.ds(r, 1), cols] * acc[i * window:(i + 1) * window]
+                )
+            return carry
+
+        lax.fori_loop(0, width // tile, columns, 0)
+
+    def sum_copy(step):
+        to = lax.rem(t + step, 4)
+        return pltpu.make_async_remote_copy(
+            src_ref=partial.at[pl.ds(to * own_pairs, own_pairs)], dst_ref=arrived.at[step - 1],
+            send_sem=sum_send.at[step - 1], recv_sem=sum_recv.at[step - 1],
+            device_id={"tensor": to}, device_id_type=MESH,
+        )
+
+    def low_copy(step, owner):
+        ref = low.at[pl.ds(owner * own_pairs, own_pairs)]
+        return pltpu.make_async_remote_copy(
+            src_ref=ref, dst_ref=ref,
+            send_sem=low_send.at[step - 1], recv_sem=low_recv.at[step - 1],
+            device_id={"tensor": lax.rem(t + step, 4)}, device_id_type=MESH,
+        )
+
+    def project_down():
+        def one(r):
+            x = attention[t, pl.ds(pl.multiple_of(r * window, window), window), :]
+            return lax.dot_general(
+                x, down[index[r]], (((1,), (1,)), ((), ())), preferred_element_type=jnp.float32
+            )
+
+        def pair(p, carry):
+            partial[p] = jnp.concatenate([one(2 * p), one(2 * p + 1)], axis=1)
+            return carry
+
+        lax.fori_loop(0, pairs, pair, 0)
+
+    start_own(0)
+    for q in range(PARTS):
+        across_copy(q).start()
+        near_copy(q).start()
+    gate[...] = gate_in[...].astype(jnp.float32)
+
+    for j in range(PIECES):
+        relay(0, 0, j)
+    relay_attention(0)
+    for j in range(PIECES):
+        relay(0, 1, j)
+    relay_attention(1)
+    start_own(1)
+    local[0].wait()
+    local[2].wait()
+    local[3].wait()
+    base_part(0)
+    for hop in range(2, hops):
+        for j in range(PIECES):
+            relay(0, hop, j)
+    base_part(1)
+    relay_attention(2)
+
+    local[1].wait()
+    await_other_group(0)
+    project_down()
+    for step in (1, 2, 3):
+        sum_copy(step).start()
+    for j in range(PIECES):
+        relay(1, 0, j)
+    for step in (1, 2, 3):
+        sum_copy(step).wait_recv()
+    own = pl.ds(t * own_pairs, own_pairs)
+    low[own] = (partial[own] + arrived[0] + arrived[1] + arrived[2]).astype(jnp.bfloat16)
+    for step in (1, 2, 3):
+        low_copy(step, t).start()
+    for j in range(PIECES):
+        relay(1, 1, j)
+    relay_attention(3)
+    base_part(2)
+    for hop in range(2, hops):
+        for j in range(PIECES):
+            relay(1, hop, j)
+    base_part(3)
+
+    for step in (1, 2, 3):
+        low_copy(step, lax.rem(t + 4 - step, 4)).wait_recv()
+    local[4].wait()
+    await_other_group(1)
+    writes = []
+    for q in range(PARTS):
+        def pair(p, carry):
+            both = low[p]
+            for i in (0, 1):
+                r = 2 * p + i
+                at = pl.ds(pl.multiple_of(r * window, window), window)
+                delta = jnp.dot(
+                    both[:, i * rank:(i + 1) * rank], up[index[r]], preferred_element_type=jnp.float32
+                )
+                result[at, :] = (total[at, :] + gate[pl.ds(r, 1), :] * delta).astype(result.dtype)
+            return carry
+
+        lax.fori_loop(q * pairs // PARTS, (q + 1) * pairs // PARTS, pair, 0)
+        write = pltpu.make_async_copy(result.at[part(q)], out.at[part(q)], out_sem.at[q])
+        write.start()
+        writes.append(write)
+
+    for stage in (0, 1):
+        for hop in range(hops):
+            for j in range(PIECES):
+                for way in (0, 1):
+                    @pl.when(sends(way, hop))
+                    def _():
+                        z_copy(stage, way, hop, j).wait_send()
+
+                    @pl.when(receives(way, hop))
+                    def _():
+                        y_copy(stage, way, hop, j, g).wait_send()
+    for q in range(PARTS):
+        across_copy(q).wait_send()
+        near_copy(q).wait_send()
+        pass_copy(q).wait_send()
+    for step in (1, 2, 3):
+        sum_copy(step).wait_send()
+        low_copy(step, t).wait_send()
+    for write in writes:
+        write.wait()
+
+
+def fused_body(
+    holders,
+    residual,
+    attention,
+    gate,
+    output_projection_weight,
+    adapter_down_weight,
+    adapter_up_weight,
+    request_adapter_index,
+):
+    rows, width = attention.shape
+    requests = gate.shape[0]
+    share, rank, _ = adapter_down_weight.shape
+    window = rows // requests
+    pairs = requests // 2
+    hops = holders - 1
+    bf16, f32 = jnp.bfloat16, jnp.float32
+    dma = pltpu.SemaphoreType.DMA
+    z = 4 * hops * PIECES
+    anywhere = pl.BlockSpec(memory_space=pl.ANY)
+    return pl.pallas_call(
+        functools.partial(fused_kernel, holders),
+        out_shape=jax.ShapeDtypeStruct((rows, width), bf16),
+        in_specs=[
+            pl.BlockSpec(memory_space=pltpu.SMEM),
+            pl.BlockSpec(memory_space=pltpu.VMEM),
+            anywhere, anywhere, anywhere, anywhere, anywhere,
+        ],
+        out_specs=anywhere,
+        scratch_shapes=[
+            pltpu.VMEM((4, rows, width), bf16),
+            pltpu.VMEM((4 * width, width), bf16),
+            pltpu.VMEM((holders * share, rank, width), bf16),
+            pltpu.VMEM((holders * share, rank, width), bf16),
+            pltpu.VMEM((rows, width), bf16),
+            pltpu.VMEM((requests, width), f32),
+            pltpu.VMEM((rows, width), f32),
+            pltpu.VMEM((rows, width), bf16),
+            pltpu.VMEM((pairs, window, 2 * rank), f32),
+            pltpu.VMEM((3, pairs // 4, window, 2 * rank), f32),
+            pltpu.VMEM((pairs, window, 2 * rank), bf16),
+            dma((z,)), dma((z,)), dma((z,)), dma((z,)),
+            dma((PARTS,)), dma((PARTS,)), dma((PARTS,)), dma((PARTS,)), dma((PARTS,)), dma((PARTS,)),
+            dma((3,)), dma((3,)), dma((3,)), dma((3,)),
+            dma((5,)), dma((PARTS,)),
+        ],
+        compiler_params=pltpu.CompilerParams(
+            collective_id=0, has_side_effects=True, vmem_limit_bytes=56 * 2**20
+        ),
+        cost_estimate=pl.CostEstimate(
+            flops=2 * rows * width * (4 * width + 2 * rank), bytes_accessed=24 * 2**20, transcendentals=0
+        ),
+    )(
+        request_adapter_index, gate, residual, attention,
+        output_projection_weight, adapter_down_weight, adapter_up_weight,
+    )
+
+
 def solution(mesh):
     in_specs = (
         P(("groups", "dp"), "tensor"),
@@ -75,4 +472,9 @@
         P(("groups", "dp")),
     )
     out_specs = P(("groups", "dp"), "tensor")
+    holders = mesh.shape["dp"]
+    if mesh.shape["tensor"] == 4 and mesh.shape["groups"] == 2 and 2 < holders <= 8:
+        body = functools.partial(fused_body, holders)
+    else:
+        body = exchange_body
     return jax.shard_map(body, mesh=mesh, in_specs=in_specs, out_specs=out_specs, check_vma=False)

time: 224 us -> 71.9 us (0.32)
  waiting for transfers between devices: 137 us -> 0 us
  Pallas kernels: 0 us -> 69.1 us
  matrix products: 21.8 us -> 0 us
  blocking collectives: 16.6 us -> 0 us
  starting transfers between devices: 16 us -> 0 us
  local copies, waits for them, and re-layouts: 17.8 us -> 2.65 us
  between operations: 13.5 us -> 0.01 us
    all_to_all x3 -> x0, waiting for transfers between devices: 136 us -> none  [the longest x1 71.2 us: body(): lax.all_to_all(delta, 'dp', split_axis=0, concat_axis=0, tiled=True)]
    pallas_call x0 -> x1, Pallas kernels: none -> 69.1 us  [fused_body(): pl.pallas_call(functools.partial(fused_kernel, holders), out_shape=jax.Sh...]
    dot_general x5 -> x0, matrix products: 21.8 us -> none  [the longest x1 9.93 us: body(): jnp.dot(lax.all_gather(attention, 'tensor', axis=1, tiled=True), output_p...]
    psum x1 -> x0, blocking collectives: 16.6 us -> none  [body(): lax.psum(partial_low.reshape(array_shape[0], array_shape[1], array_shape[...]
    all_to_all x3 -> x0, starting transfers between devices: 16 us -> none  [the longest x1 6.32 us: body(): lax.all_to_all(wanted, 'dp', split_axis=0, concat_axis=0, tiled=True)]
    reshape x4 -> x0, local copies, waits for them, and re-layouts: 8.05 us -> none  [the longest x1 3.45 us: body(): delta_rows = gathered_back.reshape(rows, width)]
    gather x2 -> x0, local copies, waits for them, and re-layouts: 4.78 us -> none  [the longest x1 2.4 us: body(): down_matrix = jnp.take(adapter_down_weight, received_slots, axis=0)]
  transfers between devices with their start and end apart: 4 -> 0, of which waited for: 3 -> 0; matrix products, arithmetic and copies ran while one was open for 13% -> 0% of each run, Pallas kernels for 0% -> 0%
where the time goes in v1:
time: 71.9 us; the launch traced here: 71.7 us
  Pallas kernels  69.1 us (96%)
  local copies, waits for them, and re-layouts  2.65 us (4%)
    pallas_call x1, Pallas kernels, fused_body(): pl.pallas_call(functools.partial(fused_kernel, holders), out_shape=jax.Sh...  69.1 us
    unnamed x1, local copies, waits for them, and re-layouts  2.65 us

profile of v1, /device:TPU:0, one launch (start us, length us, event | category | flops | bytes accessed | tf_op | source)
XLA Modules:
  0.0 71.7 jit_solution(5252432405899811842)
XLA Ops:
  0.0 69.1 %shard_map.73 = bf16[1024,768]{1,0:T(8,128)(2,1)} custom-call(s32[16]{0:T(128)} %index.1, bf16[16,768]{1,0:T(8,128)(2,1)} %gate_in.1, bf16[1024,768]{1,0:T(8,128)(2,1)} %residual_in.1, bf16[1024,768]{1,0:T(8,128)(2,1)} %attention_in.1, bf16[3072,768]{1,0:T(8,128)(2,1)} %weight_in.1, bf16[8,64,768]{2,1,0:T(8,128)(2,1)} %down_in.1, bf16[8,64,768]{2,1,0:T(8,128)(2,1)} %up_in.1), custom_call_target="tpu_custom_call" | custom-call | flops 5033164800 | bytes 25165824 | tf_op jit(solution)/shard_map/pallas_call | solution.py:426
  69.1 2.7 %copy.9 = bf16[1024,768]{1,0:T(8,128)(2,1)} copy(bf16[1024,768]{1,0:T(8,128)(2,1)} %shard_map.73) | data formatting | bytes 3145728

commit v2 on v1

--- a/solution.py
+++ b/solution.py
@@ -75,6 +75,7 @@
 def fused_kernel(
     holders,
     index,
+    index_in,
     gate_in,
     residual_in,
     attention_in,
@@ -93,6 +94,10 @@
     partial,
     arrived,
     low,
+    guest,
+    guest_index,
+    help_out,
+    help_in,
     z_send,
     z_recv,
     y_send,
@@ -107,6 +112,10 @@
     sum_recv,
     low_send,
     low_recv,
+    more_send,
+    more_recv,
+    guest_send,
+    guest_recv,
     local_sem,
     out_sem,
 ):
@@ -129,6 +138,10 @@
     own_pairs = pairs // 4
     hops = holders - 1
     inputs, buffers = (down_in, up_in), (down, up)
+    at_end = jnp.logical_or(d == 0, d == holders - 1)
+    inside = jnp.logical_not(at_end)
+    partner = d + 1 - 2 * lax.rem(d, 2)
+    first, last = pl.ds(0, width // 2), pl.ds(width // 2, width // 2)
 
     own_block = pl.ds(d * share, share)
     local = [
@@ -181,32 +194,66 @@
     def receives(way, hop):
         return rank_on(way) > hop
 
-    def z_copy(stage, way, hop, j):
+    def at_edge(way):
+        return d == (holders - 2 if way == 0 else 1)
+
+    def cut(ref, stage, narrow):
+        return ref.at[:, :, last] if narrow else ref
+
+    def either(stage, narrow, act):
+        if stage == 1:
+            act(False)
+        else:
+            pl.when(narrow)(lambda: act(True))
+            pl.when(jnp.logical_not(narrow))(lambda: act(False))
+
+    def z_copy(stage, way, hop, j, narrow):
         sign = 1 if way == 0 else -1
         target = buffers[stage].at[place(d - sign * hop, g, j)]
         source = inputs[stage].at[pl.ds(g * half + j * piece, piece)] if hop == 0 else target
         i = slot(stage, way, hop, j)
         return pltpu.make_async_remote_copy(
-            src_ref=source, dst_ref=target, send_sem=z_send.at[i], recv_sem=z_recv.at[i],
+            src_ref=cut(source, stage, narrow), dst_ref=cut(target, stage, narrow),
+            send_sem=z_send.at[i], recv_sem=z_recv.at[i],
             device_id={"dp": d + sign}, device_id_type=MESH,
         )
 
-    def z_arrival(stage, way, hop, j):
+    def z_start(stage, way, hop, j):
+        either(stage, at_edge(way), lambda n: z_copy(stage, way, hop, j, n).start())
+
+    def z_sent(stage, way, hop, j):
+        either(stage, at_edge(way), lambda n: z_copy(stage, way, hop, j, n).wait_send())
+
+    def z_arrival(stage, way, hop, j, narrow):
         sign = 1 if way == 0 else -1
-        target = buffers[stage].at[place(d - sign * (hop + 1), g, j)]
+        target = cut(buffers[stage].at[place(d - sign * (hop + 1), g, j)], stage, narrow)
         i = slot(stage, way, hop, j)
         return pltpu.make_async_remote_copy(
             src_ref=target, dst_ref=target, send_sem=z_send.at[i], recv_sem=z_recv.at[i],
             device_id={"dp": d - sign}, device_id_type=MESH,
         )
 
-    def y_copy(stage, way, hop, j, side):
+    def y_copy(stage, way, hop, j, side, narrow):
         sign = 1 if way == 0 else -1
-        target = buffers[stage].at[place(d - sign * (hop + 1), side, j)]
+        target = cut(buffers[stage].at[place(d - sign * (hop + 1), side, j)], stage, narrow)
         i = slot(stage, way, hop, j)
         return pltpu.make_async_remote_copy(
             src_ref=target, dst_ref=target, send_sem=y_send.at[i], recv_sem=y_recv.at[i],
             device_id={"groups": 1 - g}, device_id_type=MESH,
+        )
+
+    def over_y(stage, way, hop, act):
+        if stage == 1 and hop == 0:
+            pl.when(jnp.logical_not(at_edge(way)))(lambda: act(False))
+        else:
+            either(stage, at_end, act)
+
+    def more_copy(j, holder):
+        target = up.at[place(holder, 1 - g, j)]
+        return pltpu.make_async_remote_copy(
+            src_ref=up_in.at[pl.ds((1 - g) * half + j * piece, piece)], dst_ref=target,
+            send_sem=more_send.at[j], recv_sem=more_recv.at[j],
+            device_id={"dp": holders - 1 - d}, device_id_type=MESH,
         )
 
     def start_own(stage):
@@ -214,18 +261,23 @@
             for way in (0, 1):
                 @pl.when(sends(way, 0))
                 def _():
-                    z_copy(stage, way, 0, j).start()
+                    z_start(stage, way, 0, j)
+        if stage == 1:
+            @pl.when(inside)
+            def _():
+                for j in range(PIECES):
+                    more_copy(j, d).start()
 
     def relay(stage, hop, j):
         for way in (0, 1):
             @pl.when(receives(way, hop))
             def _():
-                z_arrival(stage, way, hop, j).wait_recv()
+                either(stage, at_end, lambda n: z_arrival(stage, way, hop, j, n).wait_recv())
                 if hop + 1 < hops:
                     @pl.when(sends(way, hop + 1))
                     def _():
-                        z_copy(stage, way, hop + 1, j).start()
-                y_copy(stage, way, hop, j, g).start()
+                        z_start(stage, way, hop + 1, j)
+                over_y(stage, way, hop, lambda n: y_copy(stage, way, hop, j, g, n).start())
 
     def await_other_group(stage):
         for hop in range(hops):
@@ -233,7 +285,19 @@
                 for way in (0, 1):
                     @pl.when(receives(way, hop))
                     def _():
-                        y_copy(stage, way, hop, j, 1 - g).wait_recv()
+                        over_y(stage, way, hop, lambda n: y_copy(stage, way, hop, j, 1 - g, n).wait_recv())
+        if stage == 1:
+            @pl.when(inside)
+            def _():
+                for j in range(PIECES):
+                    more_copy(j, holders - 1 - d).wait_recv()
+
+    def guest_copy(i):
+        src, dst = [(index_in, guest_index), (attention_in.at[:, first], guest), (help_out, help_in)][i]
+        return pltpu.make_async_remote_copy(
+            src_ref=src, dst_ref=dst, send_sem=guest_send.at[i], recv_sem=guest_recv.at[i],
+            device_id={"dp": partner}, device_id_type=MESH,
+        )
 
     def part(q):
         return pl.ds(q * part_rows, part_rows)
@@ -285,11 +349,11 @@
 
         lax.fori_loop(0, width // tile, columns, 0)
 
-    def sum_copy(step):
+    def sum_copy(which, step):
         to = lax.rem(t + step, 4)
         return pltpu.make_async_remote_copy(
-            src_ref=partial.at[pl.ds(to * own_pairs, own_pairs)], dst_ref=arrived.at[step - 1],
-            send_sem=sum_send.at[step - 1], recv_sem=sum_recv.at[step - 1],
+            src_ref=partial.at[which, pl.ds(to * own_pairs, own_pairs)], dst_ref=arrived.at[which, step - 1],
+            send_sem=sum_send.at[which * 3 + step - 1], recv_sem=sum_recv.at[which * 3 + step - 1],
             device_id={"tensor": to}, device_id_type=MESH,
         )
 
@@ -301,20 +365,40 @@
             device_id={"tensor": lax.rem(t + step, 4)}, device_id_type=MESH,
         )
 
-    def project_down():
+    def project_down(which, rows_of, chosen, cols):
         def one(r):
-            x = attention[t, pl.ds(pl.multiple_of(r * window, window), window), :]
+            x = rows_of(pl.ds(pl.multiple_of(r * window, window), window))
             return lax.dot_general(
-                x, down[index[r]], (((1,), (1,)), ((), ())), preferred_element_type=jnp.float32
+                x, down[chosen[r], :, cols], (((1,), (1,)), ((), ())), preferred_element_type=jnp.float32
             )
 
         def pair(p, carry):
-            partial[p] = jnp.concatenate([one(2 * p), one(2 * p + 1)], axis=1)
+            partial[which, p] = jnp.concatenate([one(2 * p), one(2 * p + 1)], axis=1)
             return carry
 
         lax.fori_loop(0, pairs, pair, 0)
+        for step in (1, 2, 3):
+            sum_copy(which, step).start()
+
+    own = pl.ds(t * own_pairs, own_pairs)
+
+    def summed(which):
+        for step in (1, 2, 3):
+            sum_copy(which, step).wait_recv()
+        return partial[which, own] + arrived[which, 0] + arrived[which, 1] + arrived[which, 2]
+
+    def share_low(value):
+        low[own] = value.astype(jnp.bfloat16)
+        for step in (1, 2, 3):
+            low_copy(step, t).start()
 
     start_own(0)
+
+    @pl.when(at_end)
+    def _():
+        guest_copy(0).start()
+        guest_copy(1).start()
+
     for q in range(PARTS):
         across_copy(q).start()
         near_copy(q).start()
@@ -322,11 +406,10 @@
 
     for j in range(PIECES):
         relay(0, 0, j)
+    start_own(1)
     relay_attention(0)
     for j in range(PIECES):
         relay(0, 1, j)
-    relay_attention(1)
-    start_own(1)
     local[0].wait()
     local[2].wait()
     local[3].wait()
@@ -334,22 +417,33 @@
     for hop in range(2, hops):
         for j in range(PIECES):
             relay(0, hop, j)
+    relay_attention(1)
     base_part(1)
-    relay_attention(2)
 
     local[1].wait()
     await_other_group(0)
-    project_down()
-    for step in (1, 2, 3):
-        sum_copy(step).start()
+
+    @pl.when(at_end)
+    def _():
+        project_down(0, lambda at: attention[t, at, last], index, last)
+
+    @pl.when(inside)
+    def _():
+        guest_copy(0).wait_recv()
+        guest_copy(1).wait_recv()
+        project_down(1, lambda at: guest[at, :], guest_index, first)
+        project_down(0, lambda at: attention[t, at, :], index, pl.ds(0, width))
+
     for j in range(PIECES):
         relay(1, 0, j)
-    for step in (1, 2, 3):
-        sum_copy(step).wait_recv()
-    own = pl.ds(t * own_pairs, own_pairs)
-    low[own] = (partial[own] + arrived[0] + arrived[1] + arrived[2]).astype(jnp.bfloat16)
-    for step in (1, 2, 3):
-        low_copy(step, t).start()
+    relay_attention(2)
+
+    @pl.when(inside)
+    def _():
+        help_out[...] = summed(1)
+        guest_copy(2).start()
+        share_low(summed(0))
+
     for j in range(PIECES):
         relay(1, 1, j)
     relay_attention(3)
@@ -357,6 +451,12 @@
     for hop in range(2, hops):
         for j in range(PIECES):
             relay(1, hop, j)
+
+    @pl.when(at_end)
+    def _():
+        guest_copy(2).wait_recv()
+        share_low(summed(0) + help_in[...])
+
     base_part(3)
 
     for step in (1, 2, 3):
@@ -387,18 +487,32 @@
                 for way in (0, 1):
                     @pl.when(sends(way, hop))
                     def _():
-                        z_copy(stage, way, hop, j).wait_send()
+                        z_sent(stage, way, hop, j)
 
                     @pl.when(receives(way, hop))
                     def _():
-                        y_copy(stage, way, hop, j, g).wait_send()
+                        over_y(stage, way, hop, lambda n: y_copy(stage, way, hop, j, g, n).wait_send())
     for q in range(PARTS):
         across_copy(q).wait_send()
         near_copy(q).wait_send()
         pass_copy(q).wait_send()
     for step in (1, 2, 3):
-        sum_copy(step).wait_send()
+        sum_copy(0, step).wait_send()
         low_copy(step, t).wait_send()
+
+    @pl.when(at_end)
+    def _():
+        guest_copy(0).wait_send()
+        guest_copy(1).wait_send()
+
+    @pl.when(inside)
+    def _():
+        guest_copy(2).wait_send()
+        for step in (1, 2, 3):
+            sum_copy(1, step).wait_send()
+        for j in range(PIECES):
+            more_copy(j, d).wait_send()
+
     for write in writes:
         write.wait()
 
@@ -428,6 +542,7 @@
         out_shape=jax.ShapeDtypeStruct((rows, width), bf16),
         in_specs=[
             pl.BlockSpec(memory_space=pltpu.SMEM),
+            anywhere,
             pl.BlockSpec(memory_space=pltpu.VMEM),
             anywhere, anywhere, anywhere, anywhere, anywhere,
         ],
@@ -441,12 +556,17 @@
             pltpu.VMEM((requests, width), f32),
             pltpu.VMEM((rows, width), f32),
             pltpu.VMEM((rows, width), bf16),
-            pltpu.VMEM((pairs, window, 2 * rank), f32),
-            pltpu.VMEM((3, pairs // 4, window, 2 * rank), f32),
+            pltpu.VMEM((2, pairs, window, 2 * rank), f32),
+            pltpu.VMEM((2, 3, pairs // 4, window, 2 * rank), f32),
             pltpu.VMEM((pairs, window, 2 * rank), bf16),
+            pltpu.VMEM((rows, width // 2), bf16),
+            pltpu.SMEM((requests,), jnp.int32),
+            pltpu.VMEM((pairs // 4, window, 2 * rank), f32),
+            pltpu.VMEM((pairs // 4, window, 2 * rank), f32),
             dma((z,)), dma((z,)), dma((z,)), dma((z,)),
             dma((PARTS,)), dma((PARTS,)), dma((PARTS,)), dma((PARTS,)), dma((PARTS,)), dma((PARTS,)),
-            dma((3,)), dma((3,)), dma((3,)), dma((3,)),
+            dma((6,)), dma((6,)), dma((3,)), dma((3,)),
+            dma((PIECES,)), dma((PIECES,)), dma((3,)), dma((3,)),
             dma((5,)), dma((PARTS,)),
         ],
         compiler_params=pltpu.CompilerParams(
@@ -456,7 +576,7 @@
             flops=2 * rows * width * (4 * width + 2 * rank), bytes_accessed=24 * 2**20, transcendentals=0
         ),
     )(
-        request_adapter_index, gate, residual, attention,
+        request_adapter_index, request_adapter_index, gate, residual, attention,
         output_projection_weight, adapter_down_weight, adapter_up_weight,
     )
 
@@ -473,7 +593,7 @@
     )
     out_specs = P(("groups", "dp"), "tensor")
     holders = mesh.shape["dp"]
-    if mesh.shape["tensor"] == 4 and mesh.shape["groups"] == 2 and 2 < holders <= 8:
+    if mesh.shape["tensor"] == 4 and mesh.shape["groups"] == 2 and holders == 4:
         body = functools.partial(fused_body, holders)
     else:
         body = exchange_body

time: 71.9 us -> 71.9 us (level)
  no operation moved by 1% of the time
where the time goes in v2:
time: 71.9 us; the launch traced here: 71.7 us
  Pallas kernels  69.1 us (96%)
  local copies, waits for them, and re-layouts  2.65 us (4%)
    pallas_call x1, Pallas kernels, fused_body(): pl.pallas_call(functools.partial(fused_kernel, holders), out_shape=jax.Sh...  69.1 us
    unnamed x1, local copies, waits for them, and re-layouts  2.65 us

profile of v2, /device:TPU:0, one launch (start us, length us, event | category | flops | bytes accessed | tf_op | source)
XLA Modules:
  0.0 71.7 jit_solution(3542055256090032608)
XLA Ops:
  0.0 69.1 %shard_map.73 = bf16[1024,768]{1,0:T(8,128)(2,1)} custom-call(s32[16]{0:T(128)} %index_in.1, s32[16]{0:T(128)} %index_in.1, bf16[16,768]{1,0:T(8,128)(2,1)} %gate_in.1, bf16[1024,768]{1,0:T(8,128)(2,1)} %residual_in.1, bf16[1024,768]{1,0:T(8,128)(2,1)} %attention_in.1, bf16[3072,768]{1,0:T(8,128)(2,1)} %weight_in.1, bf16[8,64,768]{2,1,0:T(8,128)(2,1)} %down_in.1, ...), custom_call_target="tpu_custom_call" | custom-call | flops 5033164800 | bytes 25165824 | tf_op jit(solution)/shard_map/pallas_call | solution.py:540
  69.1 2.7 %copy.9 = bf16[1024,768]{1,0:T(8,128)(2,1)} copy(bf16[1024,768]{1,0:T(8,128)(2,1)} %shard_map.73) | data formatting | bytes 3145728

commit v3 on v2

--- a/solution.py
+++ b/solution.py
@@ -8,7 +8,7 @@
 from jax.sharding import PartitionSpec as P
 
 MESH = pl.DeviceIdType.MESH
-PIECES = 2
+PIECES = 4
 PARTS = 4
 
 
@@ -262,15 +262,10 @@
                 @pl.when(sends(way, 0))
                 def _():
                     z_start(stage, way, 0, j)
-        if stage == 1:
-            @pl.when(inside)
-            def _():
-                for j in range(PIECES):
-                    more_copy(j, d).start()
-
-    def relay(stage, hop, j):
+
+    def relay(stage, hop, j, also=lambda way: True):
         for way in (0, 1):
-            @pl.when(receives(way, hop))
+            @pl.when(jnp.logical_and(receives(way, hop), also(way)))
             def _():
                 either(stage, at_end, lambda n: z_arrival(stage, way, hop, j, n).wait_recv())
                 if hop + 1 < hops:
@@ -376,7 +371,7 @@
             partial[which, p] = jnp.concatenate([one(2 * p), one(2 * p + 1)], axis=1)
             return carry
 
-        lax.fori_loop(0, pairs, pair, 0)
+        lax.fori_loop(0, pairs, pair, 0, unroll=4)
         for step in (1, 2, 3):
             sum_copy(which, step).start()
 
@@ -406,26 +401,41 @@
 
     for j in range(PIECES):
         relay(0, 0, j)
-    start_own(1)
     relay_attention(0)
     for j in range(PIECES):
         relay(0, 1, j)
+    start_own(1)
+    relay_attention(1)
     local[0].wait()
     local[2].wait()
     local[3].wait()
+
+    @pl.when(at_end)
+    def _():
+        for j in range(PIECES):
+            relay(1, 0, j)
+        for j in range(PIECES):
+            relay(0, 2, j)
+
     base_part(0)
-    for hop in range(2, hops):
-        for j in range(PIECES):
-            relay(0, hop, j)
-    relay_attention(1)
     base_part(1)
+
+    @pl.when(inside)
+    def _():
+        for j in range(PIECES):
+            relay(1, 0, j, at_edge)
+        for j in range(PIECES):
+            more_copy(j, d).start()
 
     local[1].wait()
     await_other_group(0)
+    relay_attention(2)
 
     @pl.when(at_end)
     def _():
         project_down(0, lambda at: attention[t, at, last], index, last)
+        for j in range(PIECES):
+            relay(1, 1, j)
 
     @pl.when(inside)
     def _():
@@ -433,27 +443,25 @@
         guest_copy(1).wait_recv()
         project_down(1, lambda at: guest[at, :], guest_index, first)
         project_down(0, lambda at: attention[t, at, :], index, pl.ds(0, width))
-
-    for j in range(PIECES):
-        relay(1, 0, j)
-    relay_attention(2)
-
-    @pl.when(inside)
-    def _():
+        relay(1, 0, 0, lambda way: jnp.logical_not(at_edge(way)))
         help_out[...] = summed(1)
         guest_copy(2).start()
+        for j in range(1, PIECES):
+            relay(1, 0, j, lambda way: jnp.logical_not(at_edge(way)))
         share_low(summed(0))
 
-    for j in range(PIECES):
-        relay(1, 1, j)
     relay_attention(3)
     base_part(2)
-    for hop in range(2, hops):
-        for j in range(PIECES):
-            relay(1, hop, j)
+
+    @pl.when(inside)
+    def _():
+        for j in range(PIECES):
+            relay(1, 1, j)
 
     @pl.when(at_end)
     def _():
+        for j in range(PIECES):
+            relay(1, 2, j)
         guest_copy(2).wait_recv()
         share_low(summed(0) + help_in[...])
 
@@ -476,7 +484,7 @@
                 result[at, :] = (total[at, :] + gate[pl.ds(r, 1), :] * delta).astype(result.dtype)
             return carry
 
-        lax.fori_loop(q * pairs // PARTS, (q + 1) * pairs // PARTS, pair, 0)
+        lax.fori_loop(q * pairs // PARTS, (q + 1) * pairs // PARTS, pair, 0, unroll=True)
         write = pltpu.make_async_copy(result.at[part(q)], out.at[part(q)], out_sem.at[q])
         write.start()
         writes.append(write)

time: 71.9 us -> 69.2 us (0.962)
  Pallas kernels: 69.1 us -> 66.4 us
    pallas_call x1, Pallas kernels: 69.1 us -> 66.4 us  [fused_body(): pl.pallas_call(functools.partial(fused_kernel, holders), out_shape=jax.Sh...]
where the time goes in v3:
time: 69.2 us; the launch traced here: 69 us
  Pallas kernels  66.4 us (96%)
  local copies, waits for them, and re-layouts  2.65 us (4%)
    pallas_call x1, Pallas kernels, fused_body(): pl.pallas_call(functools.partial(fused_kernel, holders), out_shape=jax.Sh...  66.4 us
    unnamed x1, local copies, waits for them, and re-layouts  2.65 us

profile of v3, /device:TPU:0, one launch (start us, length us, event | category | flops | bytes accessed | tf_op | source)
XLA Modules:
  0.0 69.0 jit_solution(15561608655961231507)
XLA Ops:
  0.0 66.4 %shard_map.73 = bf16[1024,768]{1,0:T(8,128)(2,1)} custom-call(s32[16]{0:T(128)} %index_in.1, s32[16]{0:T(128)} %index_in.1, bf16[16,768]{1,0:T(8,128)(2,1)} %gate_in.1, bf16[1024,768]{1,0:T(8,128)(2,1)} %residual_in.1, bf16[1024,768]{1,0:T(8,128)(2,1)} %attention_in.1, bf16[3072,768]{1,0:T(8,128)(2,1)} %weight_in.1, bf16[8,64,768]{2,1,0:T(8,128)(2,1)} %down_in.1, ...), custom_call_target="tpu_custom_call" | custom-call | flops 5033164800 | bytes 25165824 | tf_op jit(solution)/shard_map/pallas_call | solution.py:548
  66.4 2.7 %copy.9 = bf16[1024,768]{1,0:T(8,128)(2,1)} copy(bf16[1024,768]{1,0:T(8,128)(2,1)} %shard_map.73) | data formatting | bytes 3145728
